TPU v7x, 32 devices: a whole 2x2x4 slice. The times are simulated.
32 devices in a mesh: groups: 2 (over x), replica: 16 (over z, y, core).
Axes of the slice: x: 2, y: 2, z: 4, core: 2. Of those that a mesh axis runs over, the one named last changes fastest.
Arguments:
- inputs: bfloat16 [2, 1024, 8192], P(None, ('groups', 'replica')), parts along dimension 1, may hold values from -6 to 6
- query_weight: bfloat16 [8192, 512], replicated, may hold values from -0.0625 to 0.0625
- key_cache: bfloat16 [1024, 128, 128], P(('groups', 'replica')), parts along dimension 0, may hold values from -1000 to 1000
- value_cache: bfloat16 [1024, 128, 128], P(('groups', 'replica')), parts along dimension 0, may hold values from -6 to 6
- cache_len: int32 [1024], P(('groups', 'replica')), parts along dimension 0, may hold values from 32 to 127
- adapter_ids: int32 [2, 1024, 1], P(None, ('groups', 'replica')), parts along dimension 1, may hold values from 0 to 15; in each aligned block of 32 rows (0 to 31, 32 to 63, ..., all dimensions but the last counted through in order) at most 2 rows name the same one
- adapter_home: int32 [16], P('replica'), may hold values from 0 to 15, each once
- shrink_pool: bfloat16 [16, 8192, 64], P('replica'), may hold values from -0.0625 to 0.0625
- expand_pool: bfloat16 [16, 64, 512], P('replica'), may hold values from -0.75 to 0.75
Outputs:
- attended: bfloat16 [2, 1024, 512], P(None, ('groups', 'replica')), parts along dimension 1
There are 2 independent parts, one for each index of `groups`. A program takes and returns all parts, laid end to end along the dimension named above; an argument that names none is the same for every part. Nothing has to cross between parts.
Inputs may be any that keep to these rules, and one draw needn't show every extreme that they name: `adapter_ids`: in the rows of one replica at one step no adapter is named more than 2 times, a bound that some adapter reaches in some of these blocks.
All inputs are finite; a program needn't handle non-finite values.
Results may differ from a plain program's by a relative error of at most 0.012.
The roundings to bfloat16 on the way count: a program that leaves them out, or rounds other values in their place, can miss the bound.
Values may be sent and summed in bfloat16 or wider, within the bound.
A program may use at most 64 MiB of HBM per device.

v0:
```python
import jax
import jax.numpy as jnp
from jax import lax
from jax.sharding import PartitionSpec as P

HEAD = 128
MOST = 2


def attention(query_vectors, key_cache, value_cache, limits):
    total_row_count = query_vectors.shape[0]
    per_head = query_vectors.reshape(total_row_count, -1, HEAD)
    scores = jnp.einsum(
        "nhd,ncd->nhc", per_head, key_cache, preferred_element_type=jnp.float32
    ) * HEAD ** (-0.5)
    positions = jnp.arange(key_cache.shape[1], dtype=jnp.int32)
    visible = positions[None, None, :] < limits[:, None, None]
    scores = jnp.where(visible, scores, -1e30)
    highest = jnp.max(scores, axis=-1, keepdims=True)
    weights = jnp.exp(scores - highest)
    weights = (weights / jnp.sum(weights, axis=-1, keepdims=True)).astype(jnp.bfloat16)
    mixed = jnp.einsum("nhc,ncd->nhd", weights, value_cache, preferred_element_type=jnp.float32)
    return mixed.astype(jnp.bfloat16).reshape(total_row_count, -1)


def routing_table(owners, peer_count, capacity):
    row_order = jnp.arange(owners.shape[0], dtype=jnp.int32)
    same_owner = (owners[:, None] == owners[None, :]) & (row_order[None, :] < row_order[:, None])
    slot_rank = jnp.sum(same_owner.astype(jnp.int32), axis=1)
    target = owners * capacity + slot_rank
    slot_ids = jnp.arange(peer_count * capacity, dtype=jnp.int32)
    return (target[:, None] == slot_ids[None, :]).astype(jnp.bfloat16)


def body(
    inputs,
    query_weight,
    key_cache,
    value_cache,
    cache_len,
    adapter_ids,
    adapter_home,
    shrink_pool,
    expand_pool,
):
    homes = lax.all_gather(adapter_home, "replica", axis=0, tiled=True)
    peer_count = lax.axis_size("replica")
    decode_step_count, total_row_count, model_width = inputs.shape
    flattened = inputs.reshape(decode_step_count * total_row_count, model_width)
    plain_query_rows = jnp.dot(flattened, query_weight, preferred_element_type=jnp.float32)
    adapter_labels = jnp.arange(homes.shape[0], dtype=jnp.int32)
    named = adapter_ids.reshape(-1)
    owners = jnp.sum(
        jnp.where(named[:, None] == adapter_labels[None, :], homes[None, :], 0), axis=1
    )
    shrink = shrink_pool[0]
    expand = expand_pool[0]
    partial_results = []
    for step_index in range(decode_step_count):
        chosen = owners[step_index * total_row_count : (step_index + 1) * total_row_count]
        routing = routing_table(chosen, peer_count, MOST)
        own_rows = flattened[step_index * total_row_count : (step_index + 1) * total_row_count]
        outgoing = jnp.dot(routing.T, own_rows, preferred_element_type=jnp.float32).astype(
            jnp.bfloat16
        )
        outgoing = outgoing.reshape(peer_count, MOST, model_width)
        low_rank = jnp.einsum(
            "skd,dr->skr",
            lax.all_to_all(outgoing, "replica", split_axis=0, concat_axis=0, tiled=True),
            shrink,
            preferred_element_type=jnp.float32,
        ).astype(jnp.bfloat16)
        answers = jnp.einsum(
            "skr,rq->skq", low_rank, expand, preferred_element_type=jnp.float32
        ).astype(jnp.bfloat16)
        returned = lax.all_to_all(answers, "replica", split_axis=0, concat_axis=0, tiled=True)
        partial_results.append(
            jnp.dot(
                routing, returned.reshape(peer_count * MOST, -1), preferred_element_type=jnp.float32
            )
        )
    adapter_correction = jnp.concatenate(partial_results, axis=0)
    query_vectors = (
        (plain_query_rows + adapter_correction)
        .astype(jnp.bfloat16)
        .reshape(decode_step_count, total_row_count, -1)
    )
    results = [
        attention(query_vectors[step_index], key_cache, value_cache, cache_len + step_index)
        for step_index in range(decode_step_count)
    ]
    return jnp.stack(results)


def solution(mesh):
    return jax.shard_map(
        body,
        mesh=mesh,
        in_specs=(
            P(None, ("groups", "replica"), None),
            P(),
            P(("groups", "replica"), None, None),
            P(("groups", "replica"), None, None),
            P(("groups", "replica")),
            P(None, ("groups", "replica"), None),
            P("replica"),
            P("replica", None, None),
            P("replica", None, None),
        ),
        out_specs=P(None, ("groups", "replica"), None),
        check_vma=False,
    )
```

profile of v0, /device:TPU:0, one launch (start us, length us, event | category | flops | bytes accessed | tf_op | source)
XLA Modules:
  0.0 90.2 jit_solution(213893319616219082)
XLA Ops:
  0.8 1.2 %dynamic-slice = u32[1]{0:T(128)} dynamic-slice(u32[32]{0:T(128)} %constant.19, u32[]{:T(128)S(6)} %add.20), dynamic_slice_sizes={1} | dynamic-slice | bytes 12
  2.1 0.8 dynamic-update-slice
  2.8 13.7 %all-reduce = s32[16]{0:T(128)S(1)} all-reduce(s32[16]{0:T(128)S(1)} %dynamic-update-slice), channel_id=1, replica_groups=mesh['groups'=2,'replica'=16] {'replica'}, use_global_device_ids=true, to_apply=%add | all-reduce | flops 16 | bytes 128
  17.0 1.3 %reduce.3 = s32[2,32]{1,0:T(2,128)S(1)} reduce(s32[2,32,1]{1,2,0:T(1,128)} %param.14, s32[]{:T(128)} %broadcast.52), dimensions={2}, to_apply=%param.14.reduce_sub_computation.3 | reduce | bytes 516 | tf_op args[5]
  18.9 1.5 %convolution_convert_fusion.1 = bf16[32,8192]{1,0:T(8,128)(2,1)S(1)} fusion(bf16[2,32,8192]{2,1,0:T(8,128)(2,1)} %param.9, s32[32]{0:T(128)S(1)} %get-tuple-element.7), kind=kOutput, calls=%fused_computation.3 | convolution fusion | flops 17040384 | bytes 1048704 | tf_op jit(solution)/shard_map/dot_general | solution.py:63
  20.4 1.2 %reshape.77 = bf16[16,2,8192]{2,1,0:T(2,128)(2,1)} reshape(bf16[32,8192]{1,0:T(8,128)(2,1)S(1)} %convolution_convert_fusion.1) | data formatting | bytes 1048576 | tf_op jit(solution)/shard_map/reshape | solution.py:66
  21.5 3.6 %all-to-all-start = ((bf16[16,2,8192]{2,1,0:T(2,128)(2,1)}), bf16[16,2,8192]{2,1,0:T(2,128)(2,1)S(1)}, u32[]{:S(2)}, u32[]{:S(2)}) async-start(bf16[16,2,8192]{2,1,0:T(2,128)(2,1)} %reshape.77), calls=%async_computation | async-start | bytes 1048576 | tf_op jit(solution)/shard_map/all_to_all | solution.py:69
  25.1 1.5 %convolution_convert_fusion = bf16[32,8192]{1,0:T(8,128)(2,1)S(1)} fusion(bf16[2,32,8192]{2,1,0:T(8,128)(2,1)} %param.9, s32[32]{0:T(128)S(1)} %get-tuple-element.8), kind=kOutput, calls=%fused_computation.2 | convolution fusion | flops 17040384 | bytes 1048704 | tf_op jit(solution)/shard_map/dot_general | solution.py:63
  26.6 1.1 %reshape.79 = bf16[16,2,8192]{2,1,0:T(2,128)(2,1)} reshape(bf16[32,8192]{1,0:T(8,128)(2,1)S(1)} %convolution_convert_fusion) | data formatting | bytes 1048576 | tf_op jit(solution)/shard_map/reshape | solution.py:66
  27.7 11.8 %all-to-all-done = bf16[16,2,8192]{2,1,0:T(2,128)(2,1)S(1)} async-done(((bf16[16,2,8192]{2,1,0:T(2,128)(2,1)}), bf16[16,2,8192]{2,1,0:T(2,128)(2,1)S(1)}, u32[]{:S(2)}, u32[]{:S(2)}) %all-to-all-start) | async-done | bytes 524320 | tf_op jit(solution)/shard_map/all_to_all | solution.py:69
  39.5 4.0 %all-to-all-start.2 = ((bf16[16,2,8192]{2,1,0:T(2,128)(2,1)}), bf16[16,2,8192]{2,1,0:T(2,128)(2,1)S(1)}, u32[]{:S(2)}, u32[]{:S(2)}) async-start(bf16[16,2,8192]{2,1,0:T(2,128)(2,1)} %reshape.79), calls=%async_computation.2 | async-start | bytes 1048576 | tf_op jit(solution)/shard_map/all_to_all | solution.py:69
  43.5 0.7 broadcast_add_fusion
  44.2 0.7 iota_compare_fusion.8
  45.0 1.5 %convolution_convert_fusion.5 = bf16[16,2,512]{2,0,1:T(8,128)(2,1)S(1)} fusion(bf16[1,8192,64]{1,2,0:T(8,128)(2,1)S(1)} %copy-done, bf16[16,2,8192]{2,1,0:T(2,128)(2,1)S(1)} %all-to-all-done, bf16[1,64,512]{2,1,0:T(8,128)(2,1)} %param.17), kind=kOutput, calls=%fused_computation.17 | convolution fusion | flops 35670016 | bytes 1671168 | tf_op jit(solution)/shard_map/skr,rq->skq/dot_general | solution.py:73
  47.2 10.8 %all-to-all-done.2 = bf16[16,2,8192]{2,1,0:T(2,128)(2,1)S(1)} async-done(((bf16[16,2,8192]{2,1,0:T(2,128)(2,1)}), bf16[16,2,8192]{2,1,0:T(2,128)(2,1)S(1)}, u32[]{:S(2)}, u32[]{:S(2)}) %all-to-all-start.2) | async-done | bytes 524320 | tf_op jit(solution)/shard_map/all_to_all | solution.py:69
  58.0 4.1 %all-to-all-start.1 = ((bf16[16,2,512]{2,1,0:T(2,128)(2,1)}), bf16[16,2,512]{2,1,0:T(2,128)(2,1)S(1)}, u32[]{:S(2)}, u32[]{:S(2)}) async-start(bf16[16,2,512]{2,1,0:T(2,128)(2,1)} %copy.21), calls=%async_computation.1 | async-start | bytes 65536 | tf_op jit(solution)/shard_map/all_to_all | solution.py:76
  62.1 1.5 %convolution_convert_fusion.4 = bf16[16,2,512]{2,0,1:T(8,128)(2,1)S(1)} fusion(bf16[1,8192,64]{1,2,0:T(8,128)(2,1)S(1)} %copy-done, bf16[16,2,8192]{2,1,0:T(2,128)(2,1)S(1)} %all-to-all-done.2, bf16[1,64,512]{2,1,0:T(8,128)(2,1)} %param.17), kind=kOutput, calls=%fused_computation.16 | convolution fusion | flops 35670016 | bytes 1671168 | tf_op jit(solution)/shard_map/skr,rq->skq/dot_general | solution.py:73
  63.6 0.6 copy.23
  64.3 4.5 %all-to-all-done.1 = bf16[16,2,512]{2,1,0:T(2,128)(2,1)S(1)} async-done(((bf16[16,2,512]{2,1,0:T(2,128)(2,1)}), bf16[16,2,512]{2,1,0:T(2,128)(2,1)S(1)}, u32[]{:S(2)}, u32[]{:S(2)}) %all-to-all-start.1) | async-done | bytes 32800 | tf_op jit(solution)/shard_map/all_to_all | solution.py:76
  68.8 3.5 %all-to-all-start.3 = ((bf16[16,2,512]{2,1,0:T(2,128)(2,1)}), bf16[16,2,512]{2,1,0:T(2,128)(2,1)S(1)}, u32[]{:S(2)}, u32[]{:S(2)}) async-start(bf16[16,2,512]{2,1,0:T(2,128)(2,1)} %copy.23), calls=%async_computation.3 | async-start | bytes 65536 | tf_op jit(solution)/shard_map/all_to_all | solution.py:76
  72.5 6.4 %all-to-all-done.3 = bf16[16,2,512]{2,1,0:T(2,128)(2,1)S(1)} async-done(((bf16[16,2,512]{2,1,0:T(2,128)(2,1)}), bf16[16,2,512]{2,1,0:T(2,128)(2,1)S(1)}, u32[]{:S(2)}, u32[]{:S(2)}) %all-to-all-start.3) | async-done | bytes 32800 | tf_op jit(solution)/shard_map/all_to_all | solution.py:76
  79.1 5.0 %fusion.2 = bf16[64,512]{1,0:T(8,128)(2,1)S(1)} fusion(bf16[64,8192]{1,0:T(8,128)(2,1)S(1)} %bitcast.37, bf16[8192,512]{1,0:T(8,128)(2,1)} %param.10, f32[32,512]{1,0:T(8,128)S(1)} %fusion.25, f32[32,512]{1,0:T(8,128)S(1)} %fusion.26), kind=kOutput, calls=%fused_computation.5 | convolution fusion | flops 536969216 | bytes 9633792 | tf_op jit(solution)/shard_map/dot_general | solution.py:50
  85.0 1.8 %convolution_convert_fusion.3 = bf16[32,4,128]{2,1,0:T(4,128)(2,1)S(1)} fusion(bf16[32,128,128]{2,1,0:T(8,128)(2,1)} %param.12, f32[32,4]{1,0:T(8,128)S(1)} %fusion.36, f32[32,4,128]{2,1,0:T(4,128)S(1)} %fusion.8), kind=kOutput, calls=%fused_computation.15 | convolution fusion | flops 4260095 | bytes 1147392 | tf_op jit(solution)/shard_map/nhc,ncd->nhd/dot_general | solution.py:22
  87.7 1.8 %convolution_convert_fusion.2 = bf16[32,4,128]{2,1,0:T(4,128)(2,1)S(1)} fusion(bf16[32,128,128]{2,1,0:T(8,128)(2,1)} %param.12, f32[32,4]{1,0:T(8,128)S(1)} %fusion.35, f32[32,4,128]{2,1,0:T(4,128)S(1)} %fusion.7), kind=kOutput, calls=%fused_computation.14 | convolution fusion | flops 4260095 | bytes 1147392 | tf_op jit(solution)/shard_map/nhc,ncd->nhd/dot_general | solution.py:22
  (29 shorter events, 4.6 us)
Async XLA Ops:
  0.0 45.0 %copy-start = (bf16[1,8192,64]{1,2,0:T(8,128)(2,1)S(1)}, bf16[1,8192,64]{1,2,0:T(8,128)(2,1)}, u32[]{:S(2)}) copy-start(bf16[1,8192,64]{1,2,0:T(8,128)(2,1)} %param.16) | copy-start | bytes 3145732
  0.0 79.1 %copy-start.1 = (bf16[2,32,8192]{2,1,0:T(8,128)(2,1)S(1)}, bf16[2,32,8192]{2,1,0:T(8,128)(2,1)}, u32[]{:S(2)}) copy-start(bf16[2,32,8192]{2,1,0:T(8,128)(2,1)} %param.9) | copy-start | bytes 3145732
  21.5 18.0 %all-to-all-start = ((bf16[16,2,8192]{2,1,0:T(2,128)(2,1)}), bf16[16,2,8192]{2,1,0:T(2,128)(2,1)S(1)}, u32[]{:S(2)}, u32[]{:S(2)}) async-start(bf16[16,2,8192]{2,1,0:T(2,128)(2,1)} %reshape.77), calls=%async_computation | async-start | bytes 1048576 | tf_op jit(solution)/shard_map/all_to_all | solution.py:69
  39.5 18.5 %all-to-all-start.2 = ((bf16[16,2,8192]{2,1,0:T(2,128)(2,1)}), bf16[16,2,8192]{2,1,0:T(2,128)(2,1)S(1)}, u32[]{:S(2)}, u32[]{:S(2)}) async-start(bf16[16,2,8192]{2,1,0:T(2,128)(2,1)} %reshape.79), calls=%async_computation.2 | async-start | bytes 1048576 | tf_op jit(solution)/shard_map/all_to_all | solution.py:69
  58.0 10.7 %all-to-all-start.1 = ((bf16[16,2,512]{2,1,0:T(2,128)(2,1)}), bf16[16,2,512]{2,1,0:T(2,128)(2,1)S(1)}, u32[]{:S(2)}, u32[]{:S(2)}) async-start(bf16[16,2,512]{2,1,0:T(2,128)(2,1)} %copy.21), calls=%async_computation.1 | async-start | bytes 65536 | tf_op jit(solution)/shard_map/all_to_all | solution.py:76
  68.8 10.1 %all-to-all-start.3 = ((bf16[16,2,512]{2,1,0:T(2,128)(2,1)}), bf16[16,2,512]{2,1,0:T(2,128)(2,1)S(1)}, u32[]{:S(2)}, u32[]{:S(2)}) async-start(bf16[16,2,512]{2,1,0:T(2,128)(2,1)} %copy.23), calls=%async_computation.3 | async-start | bytes 65536 | tf_op jit(solution)/shard_map/all_to_all | solution.py:76
  79.1 5.1 %copy-start.2 = (bf16[32,128,128]{2,1,0:T(8,128)(2,1)S(1)}, bf16[32,128,128]{2,1,0:T(8,128)(2,1)}, u32[]{:S(2)}) copy-start(bf16[32,128,128]{2,1,0:T(8,128)(2,1)} %param.11) | copy-start | bytes 3145732
where the time goes:
time: 91 us; the launch traced here: 90.2 us
  waiting for transfers between devices  33.5 us (37%)
  matrix products  16.2 us (18%)
  starting transfers between devices  15.2 us (17%)
  blocking collectives  13.7 us (15%)
  local copies, waits for them, and re-layouts  6.38 us (7%)
  other arithmetic  4.21 us (5%)
  between operations  0.96 us (1%)
    all_to_all x2, waiting for transfers between devices, body(): lax.all_to_all(outgoing, 'replica', split_axis=0, concat_axis=0, tiled=True)  22.7 us
    unnamed x1, blocking collectives  13.7 us
    all_to_all x2, waiting for transfers between devices, body(): lax.all_to_all(answers, 'replica', split_axis=0, concat_axis=0, tiled=True)  10.8 us
    all_to_all x2, starting transfers between devices, body(): lax.all_to_all(answers, 'replica', split_axis=0, concat_axis=0, tiled=True)  7.6 us
    all_to_all x2, starting transfers between devices, body(): lax.all_to_all(outgoing, 'replica', split_axis=0, concat_axis=0, tiled=True)  7.59 us
    dot_general x1, matrix products, body(): jnp.dot(flattened, query_weight, preferred_element_type=jnp.float32)  5.03 us
    dot_general x2, matrix products, attention(): jnp.einsum('nhc,ncd->nhd', weights, value_cache, preferred_element_type=j...  3.59 us
    dot_general x2, matrix products, body(): jnp.einsum('skr,rq->skq', low_rank, expand, preferred_element_type=jnp.fl...  3.04 us
  transfers between devices with their start and end apart: 4, of which 4 were waited for; matrix products, arithmetic and copies ran while one was open for 10% of the time, Pallas kernels for 0%

commit v1 on v0

v1 whole, which is shorter than its diff:
```python
import functools

import jax
import jax.numpy as jnp
from jax import lax
from jax.experimental import pallas as pl
from jax.experimental.pallas import tpu as pltpu
from jax.sharding import PartitionSpec as P

HEAD = 128
MOST = 2
MESH = pl.DeviceIdType.MESH
F32 = jnp.float32
BF16 = jnp.bfloat16


def iota(shape, axis):
    return lax.broadcasted_iota(jnp.int32, shape, axis)


def kernel(
    peers,
    steps,
    rows,
    width,
    rank,
    features,
    ctx,
    x_hbm,
    w_hbm,
    k_hbm,
    v_hbm,
    len_ref,
    ids_ref,
    home_ref,
    shrink_hbm,
    expand_ref,
    o_ref,
    x,
    w,
    k,
    v,
    shrink,
    wide,
    home_src,
    homes,
    out,
    inbox,
    ans_out,
    ans_in,
    base,
    limits,
    mixed,
    local_sem,
    w_sem,
    home_send,
    home_recv,
    row_send,
    row_recv,
    ans_send,
    ans_recv,
):
    me = lax.axis_index("replica")
    heads = features // HEAD
    parts = 16 // MOST
    cols = width // parts
    per_row = steps * heads
    half = peers // 2
    w_parts = w_sem.shape[0]
    w_rows = width // w_parts

    def offset(i):
        return lax.rem(peers // 2 + (1 - 2 * lax.rem(i, 2)) * ((i + 1) // 2) + peers, peers)

    def target(i):
        return lax.rem(me + offset(i), peers)

    def source(i):
        return lax.rem(me - offset(i) + peers, peers)

    def w_copy(c):
        piece = pl.ds(c * w_rows, w_rows)
        return pltpu.make_async_copy(w_hbm.at[piece], w.at[piece], w_sem.at[c])

    x_copy = pltpu.make_async_copy(x_hbm, x, local_sem.at[0])
    shrink_copy = pltpu.make_async_copy(shrink_hbm, shrink, local_sem.at[1])
    k_copy = pltpu.make_async_copy(k_hbm, k, local_sem.at[2])
    v_copy = pltpu.make_async_copy(v_hbm, v, local_sem.at[3])

    x_copy.start()
    barrier = pltpu.get_barrier_semaphore()

    @pl.loop(0, peers - 1)
    def _(i):
        pl.semaphore_signal(barrier, inc=1, device_id={"replica": target(i)}, device_id_type=MESH)

    for c in range(w_parts):
        w_copy(c).start()
    shrink_copy.start()
    k_copy.start()
    v_copy.start()
    home_src[...] = jnp.full(home_src.shape, home_ref[0], jnp.int32)
    homes[me] = home_src[...]

    def home_copy(i, slot):
        return pltpu.make_async_remote_copy(
            src_ref=home_src,
            dst_ref=homes.at[slot],
            send_sem=home_send.at[i],
            recv_sem=home_recv.at[slot],
            device_id={"replica": target(i)},
            device_id_type=MESH,
        )

    pl.semaphore_wait(barrier, peers - 1)

    @pl.loop(0, peers - 1)
    def _(i):
        home_copy(i, me).start()

    total = steps * rows
    ids_col = ids_ref[...].reshape(total, 1).astype(F32)

    def along(col, index):
        return jnp.sum(jnp.where(iota((total, index.shape[1]), 0) == index, col, 0.0), axis=0, keepdims=True)

    ids_row = along(ids_col, iota((1, total), 1))
    before = (iota((total, total), 1) < iota((total, total), 0)) & (
        iota((total, total), 1) // rows == iota((total, total), 0) // rows
    )
    place_col = jnp.sum(jnp.where(before & (ids_row == ids_col), 1.0, 0.0), axis=1, keepdims=True)
    lanes = iota((1, parts * rows), 1)
    pack_ids = [along(ids_col, lanes % rows + s * rows) for s in range(steps)]
    pack_place = [along(place_col, lanes % rows + s * rows) for s in range(steps)]
    block = iota((peers * 16, 1), 0)
    pack_target = target(block // 16)
    fits = [
        (block % parts == lanes // rows) & ((block // parts) % MOST == pack_place[s].astype(jnp.int32))
        for s in range(steps)
    ]
    x_copy.wait()

    @pl.loop(0, peers - 1)
    def _(i):
        home_copy(i, source(i)).wait_recv()

    home_col = jnp.max(homes[...], axis=1)[:, 0:1].astype(F32)

    def owner_of(ids):
        named = iota((peers, ids.shape[1]), 0) == ids.astype(jnp.int32)
        return jnp.sum(jnp.where(named, home_col, 0.0), axis=0, keepdims=True).astype(jnp.int32)

    def row_copy(s, i):
        place = pl.ds(s * 16, 16)
        return pltpu.make_async_remote_copy(
            src_ref=out.at[i, place],
            dst_ref=inbox.at[i, place],
            send_sem=row_send.at[s, i],
            recv_sem=row_recv.at[s, i],
            device_id={"replica": target(i)},
            device_id_type=MESH,
        )

    for s in range(steps):
        routing = jnp.where(fits[s] & (pack_target == owner_of(pack_ids[s])), 1.0, 0.0).astype(BF16)
        tall = jnp.concatenate([x[s, :, c * cols : (c + 1) * cols] for c in range(parts)], axis=0)
        packed = jnp.dot(routing, tall, preferred_element_type=F32).astype(BF16)
        packed = packed.reshape(peers, 16, cols)
        out[:, s * 16 : (s + 1) * 16, :] = packed
        inbox[peers - 1, s * 16 : (s + 1) * 16, :] = packed[peers - 1]

        @pl.loop(0, peers - 1)
        def _(i):
            row_copy(s, i).start()

    q_lanes = iota((1, rows * per_row), 1)
    q_rows = q_lanes // per_row + ((q_lanes // heads) % steps) * rows
    q_owner = owner_of(along(ids_col, q_rows))
    q_place = along(place_col, q_rows).astype(jnp.int32)
    a_rows = iota((peers * steps * MOST * heads, 1), 0)
    per_peer = steps * MOST * heads
    back = (
        (target(a_rows // per_peer) == q_owner)
        & ((a_rows // (MOST * heads)) % steps == (q_lanes // heads) % steps)
        & ((a_rows // heads) % MOST == q_place)
        & (a_rows % heads == q_lanes % heads)
    )
    back = jnp.transpose(jnp.where(back, 1.0, 0.0)).astype(BF16)

    flat = jnp.zeros((total, features), F32)
    for c in range(w_parts):
        w_copy(c).wait()
        piece = x[:, :, c * w_rows : (c + 1) * w_rows].reshape(total, w_rows)
        flat = flat + jnp.dot(piece, w[c * w_rows : (c + 1) * w_rows], preferred_element_type=F32)
    for s in range(steps):
        for h in range(heads):
            base[pl.ds(s * heads + h, rows, stride=per_row), :] = flat[
                s * rows : (s + 1) * rows, h * HEAD : (h + 1) * HEAD
            ]
    step_of = iota((per_row, ctx), 0) // heads
    for t in range(rows):
        limits[t] = step_of + len_ref[t]
    shrink_copy.wait()
    for c in range(0, parts, 2):
        wide[:, c * rank : (c + 2) * rank] = jnp.concatenate(
            [shrink[0, c * cols : (c + 1) * cols], shrink[0, (c + 1) * cols : (c + 2) * cols]], axis=1
        )
    expand = expand_ref[0]
    expand_tall = jnp.concatenate([expand[:, h * HEAD : (h + 1) * HEAD] for h in range(heads)], axis=0)
    k_copy.wait()
    v_copy.wait()

    g_rows = half * 16
    own_part = iota((g_rows, parts * rank), 0) % parts == iota((g_rows, parts * rank), 1) // rank

    def low_rank(s, g):
        block = inbox[g * half : (g + 1) * half, s * 16 : (s + 1) * 16, :].reshape(g_rows, cols)
        full = jnp.dot(block, wide[...], preferred_element_type=F32)
        full = jnp.where(own_part, full, 0.0).reshape(g_rows // parts, parts, parts * rank)
        full = jnp.sum(full, axis=1)
        while full.shape[1] > 2 * rank:
            full = full[:, : full.shape[1] // 2] + full[:, full.shape[1] // 2 :]
        return (full + pltpu.roll(full, rank, 1)).astype(BF16)

    def wait_rows(s, g):
        @pl.loop(g * half, min((g + 1) * half, peers - 1))
        def _(i):
            row_copy(s, i).wait_recv()

    def answer_copy(i, to):
        return pltpu.make_async_remote_copy(
            src_ref=ans_out.at[i],
            dst_ref=ans_in.at[i],
            send_sem=ans_send.at[i],
            recv_sem=ans_recv.at[i],
            device_id={"replica": to},
            device_id_type=MESH,
        )

    lows = {}
    r_rows = half * per_peer
    r_from = iota((r_rows, steps * half * MOST), 1)
    r_to = iota((r_rows, steps * half * MOST), 0)
    spread = (
        ((r_to // (MOST * heads)) % steps == r_from // (half * MOST))
        & (r_to // per_peer == (r_from // MOST) % half)
        & ((r_to // heads) % MOST == r_from % MOST)
    )
    spread = jnp.where(spread, 1.0, 0.0).astype(BF16)
    own_head = iota((r_rows, heads * rank), 0) % heads == iota((r_rows, heads * rank), 1) // rank
    for s in range(steps):
        for g in range(2):
            wait_rows(s, g)
            lows[s, g] = low_rank(s, g)
            if s < steps - 1:
                continue
            low = jnp.concatenate([lows[q, g] for q in range(steps)], axis=0)
            low = jnp.concatenate([low] * (heads // 2), axis=1)
            low = jnp.dot(spread, low, preferred_element_type=F32)
            low = jnp.where(own_head, low, 0.0).astype(BF16)
            answer = jnp.dot(low, expand_tall, preferred_element_type=F32).astype(BF16)
            answer = answer.reshape(half, per_peer, HEAD)
            ans_out[g * half : (g + 1) * half] = answer
            if g == 1:
                ans_in[peers - 1] = answer[half - 1]

            @pl.loop(g * half, min((g + 1) * half, peers - 1))
            def _(i):
                answer_copy(i, source(i)).start()

    @pl.loop(0, peers - 1)
    def _(i):
        answer_copy(i, source(i)).wait_recv()

    delta = jnp.dot(back, ans_in[...].reshape(peers * per_peer, HEAD), preferred_element_type=F32)
    query = (base[...] + delta).astype(BF16).reshape(rows, per_row, HEAD)
    scores = lax.dot_general(query, k[...], (((2,), (2,)), ((0,), (0,))), preferred_element_type=F32)
    scores = scores * HEAD ** (-0.5)
    scores = jnp.where(iota((rows, per_row, ctx), 2) < limits[...], scores, -1e30)
    weights = jnp.exp(scores - jnp.max(scores, axis=-1, keepdims=True))
    weights = (weights / jnp.sum(weights, axis=-1, keepdims=True)).astype(BF16)
    result = lax.dot_general(weights, v[...], (((2,), (1,)), ((0,), (0,))), preferred_element_type=F32)
    mixed[...] = result.reshape(rows * per_row, HEAD)
    for s in range(steps):
        for h in range(heads):
            o_ref[s, :, h * HEAD : (h + 1) * HEAD] = mixed[
                pl.ds(s * heads + h, rows, stride=per_row), :
            ].astype(BF16)

    @pl.loop(0, peers - 1)
    def _(i):
        home_copy(i, me).wait_send()
        for s in range(steps):
            row_copy(s, i).wait_send()
        answer_copy(i, source(i)).wait_send()


def body(inputs, query_weight, key_cache, value_cache, cache_len, ids, home, shrink_pool, expand_pool):
    peers = lax.axis_size("replica")
    steps, rows, width = inputs.shape
    features = query_weight.shape[1]
    rank = shrink_pool.shape[2]
    ctx = key_cache.shape[1]
    heads = features // HEAD
    cols = width * MOST // 16
    per_row = steps * heads
    vmem = pl.BlockSpec(memory_space=pltpu.VMEM)
    smem = pl.BlockSpec(memory_space=pltpu.SMEM)
    hbm = pl.BlockSpec(memory_space=pl.ANY)
    dma = pltpu.SemaphoreType.DMA
    return pl.pallas_call(
        functools.partial(kernel, peers, steps, rows, width, rank, features, ctx),
        out_shape=jax.ShapeDtypeStruct((steps, rows, features), BF16),
        in_specs=[hbm, hbm, hbm, hbm, smem, vmem, smem, hbm, vmem],
        out_specs=vmem,
        scratch_shapes=[
            pltpu.VMEM(inputs.shape, BF16),
            pltpu.VMEM(query_weight.shape, BF16),
            pltpu.VMEM(key_cache.shape, BF16),
            pltpu.VMEM(value_cache.shape, BF16),
            pltpu.VMEM(shrink_pool.shape, BF16),
            pltpu.VMEM((cols, rank * 16 // MOST), BF16),
            pltpu.VMEM((8, 128), jnp.int32),
            pltpu.VMEM((peers, 8, 128), jnp.int32),
            pltpu.VMEM((peers, steps * 16, cols), BF16),
            pltpu.VMEM((peers, steps * 16, cols), BF16),
            pltpu.VMEM((peers, steps * MOST * heads, HEAD), BF16),
            pltpu.VMEM((peers, steps * MOST * heads, HEAD), BF16),
            pltpu.VMEM((rows * per_row, HEAD), F32),
            pltpu.VMEM((rows, per_row, ctx), jnp.int32),
            pltpu.VMEM((rows * per_row, HEAD), F32),
            dma((4,)),
            dma((8,)),
            dma((peers,)),
            dma((peers,)),
            dma((steps, peers)),
            dma((steps, peers)),
            dma((peers,)),
            dma((peers,)),
        ],
        compiler_params=pltpu.CompilerParams(
            collective_id=0, has_side_effects=True, vmem_limit_bytes=48 * 2**20
        ),
    )(inputs, query_weight, key_cache, value_cache, cache_len, ids, home, shrink_pool, expand_pool)


def solution(mesh):
    return jax.shard_map(
        body,
        mesh=mesh,
        in_specs=(
            P(None, ("groups", "replica"), None),
            P(),
            P(("groups", "replica"), None, None),
            P(("groups", "replica"), None, None),
            P(("groups", "replica")),
            P(None, ("groups", "replica"), None),
            P("replica"),
            P("replica", None, None),
            P("replica", None, None),
        ),
        out_specs=P(None, ("groups", "replica"), None),
        check_vma=False,
    )
```

time: 91 us -> 52.1 us (0.57)
  Pallas kernels: 0 us -> 42.5 us
  waiting for transfers between devices: 33.5 us -> 0 us
  matrix products: 16.2 us -> 0 us
  starting transfers between devices: 15.2 us -> 0 us
  blocking collectives: 13.7 us -> 0 us
  other arithmetic: 4.21 us -> 0 us
  local copies, waits for them, and re-layouts: 6.38 us -> 8.58 us
    pallas_call x0 -> x1, Pallas kernels: none -> 42.5 us  [body(): pl.pallas_call(functools.partial(kernel, peers, steps, rows, width, rank,...]
    all_to_all x4 -> x0, waiting for transfers between devices: 33.5 us -> none  [the longest x2 22.7 us: body(): lax.all_to_all(outgoing, 'replica', split_axis=0, concat_axis=0, tiled=True)]
    dot_general x11 -> x0, matrix products: 16.2 us -> none  [the longest x1 5.03 us: body(): jnp.dot(flattened, query_weight, preferred_element_type=jnp.float32)]
    all_to_all x4 -> x0, starting transfers between devices: 15.2 us -> none  [the longest x2 7.6 us: body(): lax.all_to_all(answers, 'replica', split_axis=0, concat_axis=0, tiled=True)]
    unnamed x1 -> x0, blocking collectives: 13.7 us -> none
    unnamed x10 -> x13, local copies, waits for them, and re-layouts: 2.52 us -> 8.58 us
    reshape x4 -> x0, local copies, waits for them, and re-layouts: 2.32 us -> none  [the longest x2 2.28 us: body(): outgoing = outgoing.reshape(peer_count, MOST, model_width)]
    unnamed x1 -> x0, other arithmetic: 1.34 us -> none
  transfers between devices with their start and end apart: 4 -> 0, of which waited for: 4 -> 0; matrix products, arithmetic and copies ran while one was open for 10% -> 0% of each run, Pallas kernels for 0% -> 0%
where the time goes in v1:
time: 52.1 us; the launch traced here: 51.8 us
  Pallas kernels  42.5 us (82%)
  local copies, waits for them, and re-layouts  8.58 us (16%)
  between operations  0.68 us (1%)
    pallas_call x1, Pallas kernels, body(): pl.pallas_call(functools.partial(kernel, peers, steps, rows, width, rank,...  42.5 us
    unnamed x13, local copies, waits for them, and re-layouts  8.58 us

profile of v1, /device:TPU:0, one launch (start us, length us, event | category | flops | bytes accessed | tf_op | source)
XLA Modules:
  0.0 51.8 jit_solution(3727949775468788374)
XLA Ops:
  0.7 0.8 %copy.10.ids_ref = s32[2,32,1]{2,1,0:T(8,128)S(1)} copy(s32[2,32,1]{1,2,0:T(1,128)} %param.14) | data formatting | bytes 512 | tf_op args[5]
  1.4 2.0 %copy.11.shrink_hbm = bf16[1,8192,64]{2,1,0:T(8,128)(2,1)S(1)} copy(bf16[1,8192,64]{1,2,0:T(8,128)(2,1)} %param.16) | data formatting | bytes 2097152 | tf_op args[7]
  3.5 0.0 copy-start
  3.5 1.2 %copy-done = bf16[2,32,8192]{2,1,0:T(8,128)(2,1)S(1)} copy-done((bf16[2,32,8192]{2,1,0:T(8,128)(2,1)S(1)}, bf16[2,32,8192]{2,1,0:T(8,128)(2,1)}, u32[]{:S(2)}) %copy-start) | copy-done | bytes 1048600
  4.7 0.0 copy-start.1
  4.7 1.2 %copy-done.1 = bf16[32,128,128]{2,1,0:T(8,128)(2,1)S(1)} copy-done((bf16[32,128,128]{2,1,0:T(8,128)(2,1)S(1)}, bf16[32,128,128]{2,1,0:T(8,128)(2,1)}, u32[]{:S(2)}) %copy-start.1) | copy-done | bytes 1048600
  5.9 0.0 copy-start.2
  5.9 1.2 %copy-done.2 = bf16[32,128,128]{2,1,0:T(8,128)(2,1)S(1)} copy-done((bf16[32,128,128]{2,1,0:T(8,128)(2,1)S(1)}, bf16[32,128,128]{2,1,0:T(8,128)(2,1)}, u32[]{:S(2)}) %copy-start.2) | copy-done | bytes 1048600
  7.1 0.0 copy-start.3
  7.1 0.8 %copy-done.3 = bf16[1,64,512]{2,1,0:T(8,128)(2,1)S(1)} copy-done((bf16[1,64,512]{2,1,0:T(8,128)(2,1)S(1)}, bf16[1,64,512]{2,1,0:T(8,128)(2,1)}, u32[]{:S(2)}) %copy-start.3) | copy-done | bytes 65560
  8.0 0.0 copy-start.4
  8.0 0.7 %copy-done.4 = s32[32]{0:T(128)S(1)} copy-done((s32[32]{0:T(128)S(1)}, s32[32]{0:T(128)}, u32[]{:S(2)}) %copy-start.4) | copy-done | bytes 152
  8.6 42.5 %shard_map.91 = bf16[2,32,512]{2,1,0:T(8,128)(2,1)S(1)} custom-call(bf16[2,32,8192]{2,1,0:T(8,128)(2,1)S(1)} %copy-done, bf16[8192,512]{1,0:T(8,128)(2,1)} %w_hbm.1, bf16[32,128,128]{2,1,0:T(8,128)(2,1)S(1)} %copy-done.1, bf16[32,128,128]{2,1,0:T(8,128)(2,1)S(1)} %copy-done.2, s32[32]{0:T(128)S(1)} %copy-done.4, s32[2,32,1]{2,1,0:T(8,128)S(1)} %copy.10.ids_ref, ...), custom_call_target="tpu_custom_call" | custom-call | tf_op jit(solution)/shard_map/pallas_call | solution.py:311
  51.1 0.6 %copy.14 = bf16[2,32,512]{2,1,0:T(8,128)(2,1)} copy(bf16[2,32,512]{2,1,0:T(8,128)(2,1)S(1)} %shard_map.91) | data formatting | bytes 131072
Async XLA Ops:
  3.5 1.2 %copy-start = (bf16[2,32,8192]{2,1,0:T(8,128)(2,1)S(1)}, bf16[2,32,8192]{2,1,0:T(8,128)(2,1)}, u32[]{:S(2)}) copy-start(bf16[2,32,8192]{2,1,0:T(8,128)(2,1)} %x_hbm.1) | copy-start | bytes 3145732
  4.7 1.2 %copy-start.1 = (bf16[32,128,128]{2,1,0:T(8,128)(2,1)S(1)}, bf16[32,128,128]{2,1,0:T(8,128)(2,1)}, u32[]{:S(2)}) copy-start(bf16[32,128,128]{2,1,0:T(8,128)(2,1)} %k_hbm.1) | copy-start | bytes 3145732
  5.9 1.2 %copy-start.2 = (bf16[32,128,128]{2,1,0:T(8,128)(2,1)S(1)}, bf16[32,128,128]{2,1,0:T(8,128)(2,1)}, u32[]{:S(2)}) copy-start(bf16[32,128,128]{2,1,0:T(8,128)(2,1)} %v_hbm.1) | copy-start | bytes 3145732
  7.1 0.8 %copy-start.3 = (bf16[1,64,512]{2,1,0:T(8,128)(2,1)S(1)}, bf16[1,64,512]{2,1,0:T(8,128)(2,1)}, u32[]{:S(2)}) copy-start(bf16[1,64,512]{2,1,0:T(8,128)(2,1)} %expand_ref.1) | copy-start | bytes 196612
  8.0 0.7 %copy-start.4 = (s32[32]{0:T(128)S(1)}, s32[32]{0:T(128)}, u32[]{:S(2)}) copy-start(s32[32]{0:T(128)} %len_ref.1) | copy-start | bytes 388

commit v2 on v1

--- a/solution.py
+++ b/solution.py
@@ -30,17 +30,21 @@
     w_hbm,
     k_hbm,
     v_hbm,
-    len_ref,
-    ids_ref,
-    home_ref,
+    len_hbm,
+    ids_hbm,
+    home_hbm,
     shrink_hbm,
-    expand_ref,
+    expand_hbm,
     o_ref,
     x,
     w,
     k,
     v,
+    len_ref,
+    ids_ref,
+    home_ref,
     shrink,
+    expand_ref,
     wide,
     home_src,
     homes,
@@ -87,6 +91,13 @@
     k_copy = pltpu.make_async_copy(k_hbm, k, local_sem.at[2])
     v_copy = pltpu.make_async_copy(v_hbm, v, local_sem.at[3])
 
+    home_local = pltpu.make_async_copy(home_hbm, home_ref, local_sem.at[4])
+    ids_copy = pltpu.make_async_copy(ids_hbm, ids_ref, local_sem.at[5])
+    len_copy = pltpu.make_async_copy(len_hbm, len_ref, local_sem.at[6])
+    expand_copy = pltpu.make_async_copy(expand_hbm, expand_ref, local_sem.at[7])
+
+    home_local.start()
+    ids_copy.start()
     x_copy.start()
     barrier = pltpu.get_barrier_semaphore()
 
@@ -99,6 +110,9 @@
     shrink_copy.start()
     k_copy.start()
     v_copy.start()
+    len_copy.start()
+    expand_copy.start()
+    home_local.wait()
     home_src[...] = jnp.full(home_src.shape, home_ref[0], jnp.int32)
     homes[me] = home_src[...]
 
@@ -119,7 +133,15 @@
         home_copy(i, me).start()
 
     total = steps * rows
-    ids_col = ids_ref[...].reshape(total, 1).astype(F32)
+    ids_copy.wait()
+    same = iota((rows, rows), 0) == iota((rows, rows), 1)
+    ids_col = jnp.concatenate(
+        [
+            jnp.sum(jnp.where(same, ids_ref[s].astype(F32), 0.0), axis=1, keepdims=True)
+            for s in range(steps)
+        ],
+        axis=0,
+    )
 
     def along(col, index):
         return jnp.sum(jnp.where(iota((total, index.shape[1]), 0) == index, col, 0.0), axis=0, keepdims=True)
@@ -198,13 +220,13 @@
                 s * rows : (s + 1) * rows, h * HEAD : (h + 1) * HEAD
             ]
     step_of = iota((per_row, ctx), 0) // heads
+    len_copy.wait()
     for t in range(rows):
         limits[t] = step_of + len_ref[t]
     shrink_copy.wait()
-    for c in range(0, parts, 2):
-        wide[:, c * rank : (c + 2) * rank] = jnp.concatenate(
-            [shrink[0, c * cols : (c + 1) * cols], shrink[0, (c + 1) * cols : (c + 2) * cols]], axis=1
-        )
+    for c in range(parts):
+        wide[c * rank : (c + 1) * rank] = shrink[0, :, c * cols : (c + 1) * cols]
+    expand_copy.wait()
     expand = expand_ref[0]
     expand_tall = jnp.concatenate([expand[:, h * HEAD : (h + 1) * HEAD] for h in range(heads)], axis=0)
     k_copy.wait()
@@ -215,7 +237,7 @@
 
     def low_rank(s, g):
         block = inbox[g * half : (g + 1) * half, s * 16 : (s + 1) * 16, :].reshape(g_rows, cols)
-        full = jnp.dot(block, wide[...], preferred_element_type=F32)
+        full = lax.dot_general(block, wide[...], (((1,), (1,)), ((), ())), preferred_element_type=F32)
         full = jnp.where(own_part, full, 0.0).reshape(g_rows // parts, parts, parts * rank)
         full = jnp.sum(full, axis=1)
         while full.shape[1] > 2 * rank:
@@ -305,21 +327,24 @@
     cols = width * MOST // 16
     per_row = steps * heads
     vmem = pl.BlockSpec(memory_space=pltpu.VMEM)
-    smem = pl.BlockSpec(memory_space=pltpu.SMEM)
-    hbm = pl.BlockSpec(memory_space=pl.ANY)
+    hbm = pl.BlockSpec(memory_space=pltpu.HBM)
     dma = pltpu.SemaphoreType.DMA
     return pl.pallas_call(
         functools.partial(kernel, peers, steps, rows, width, rank, features, ctx),
         out_shape=jax.ShapeDtypeStruct((steps, rows, features), BF16),
-        in_specs=[hbm, hbm, hbm, hbm, smem, vmem, smem, hbm, vmem],
+        in_specs=[hbm] * 9,
         out_specs=vmem,
         scratch_shapes=[
             pltpu.VMEM(inputs.shape, BF16),
             pltpu.VMEM(query_weight.shape, BF16),
             pltpu.VMEM(key_cache.shape, BF16),
             pltpu.VMEM(value_cache.shape, BF16),
-            pltpu.VMEM(shrink_pool.shape, BF16),
-            pltpu.VMEM((cols, rank * 16 // MOST), BF16),
+            pltpu.SMEM(cache_len.shape, jnp.int32),
+            pltpu.VMEM((steps, 1, rows), jnp.int32),
+            pltpu.SMEM(home.shape, jnp.int32),
+            pltpu.VMEM((1, rank, width), BF16),
+            pltpu.VMEM(expand_pool.shape, BF16),
+            pltpu.VMEM((rank * 16 // MOST, cols), BF16),
             pltpu.VMEM((8, 128), jnp.int32),
             pltpu.VMEM((peers, 8, 128), jnp.int32),
             pltpu.VMEM((peers, steps * 16, cols), BF16),
@@ -329,7 +354,7 @@
             pltpu.VMEM((rows * per_row, HEAD), F32),
             pltpu.VMEM((rows, per_row, ctx), jnp.int32),
             pltpu.VMEM((rows * per_row, HEAD), F32),
-            dma((4,)),
+            dma((8,)),
             dma((8,)),
             dma((peers,)),
             dma((peers,)),
@@ -339,9 +364,19 @@
             dma((peers,)),
         ],
         compiler_params=pltpu.CompilerParams(
-            collective_id=0, has_side_effects=True, vmem_limit_bytes=48 * 2**20
+            collective_id=0, has_side_effects=True, vmem_limit_bytes=60 * 2**20
         ),
-    )(inputs, query_weight, key_cache, value_cache, cache_len, ids, home, shrink_pool, expand_pool)
+    )(
+        inputs,
+        query_weight,
+        key_cache,
+        value_cache,
+        cache_len,
+        jnp.swapaxes(ids, 1, 2),
+        home,
+        jnp.swapaxes(shrink_pool, 1, 2),
+        expand_pool,
+    )
 
 
 def solution(mesh):

time: 52.1 us -> 45.2 us (0.87)
  local copies, waits for them, and re-layouts: 8.58 us -> 1.47 us
    unnamed x13 -> x1, local copies, waits for them, and re-layouts: 8.58 us -> 1.47 us
where the time goes in v2:
time: 45.2 us; the launch traced here: 45.1 us
  Pallas kernels  42.9 us (95%)
  local copies, waits for them, and re-layouts  1.47 us (3%)
  between operations  0.66 us (1%)
    pallas_call x1, Pallas kernels, body(): pl.pallas_call(functools.partial(kernel, peers, steps, rows, width, rank,...  42.9 us
    unnamed x1, local copies, waits for them, and re-layouts  1.47 us

profile of v2, /device:TPU:0, one launch (start us, length us, event | category | flops | bytes accessed | tf_op | source)
XLA Modules:
  0.0 45.1 jit_solution(7761490986361019297)
XLA Ops:
  0.7 42.9 %shard_map.91 = bf16[2,32,512]{2,1,0:T(8,128)(2,1)} custom-call(bf16[2,32,8192]{2,1,0:T(8,128)(2,1)} %x_hbm.1, bf16[8192,512]{1,0:T(8,128)(2,1)} %w_hbm.1, bf16[32,128,128]{2,1,0:T(8,128)(2,1)} %k_hbm.1, bf16[32,128,128]{2,1,0:T(8,128)(2,1)} %v_hbm.1, s32[32]{0:T(128)} %len_hbm.1, s32[2,1,32]{2,1,0:T(1,128)} %bitcast.5, s32[1]{0:T(128)S(6)} %copy.12.home_hbm, ...), custom_call_target="tpu_custom_call" | custom-call | tf_op jit(solution)/shard_map/pallas_call | solution.py:332
  43.6 1.5 %copy.13 = bf16[2,32,512]{2,1,0:T(8,128)(2,1)} copy(bf16[2,32,512]{2,1,0:T(8,128)(2,1)} %shard_map.91) | data formatting | bytes 131072

commit v3 on v2

--- a/solution.py
+++ b/solution.py
@@ -96,22 +96,16 @@
     len_copy = pltpu.make_async_copy(len_hbm, len_ref, local_sem.at[6])
     expand_copy = pltpu.make_async_copy(expand_hbm, expand_ref, local_sem.at[7])
 
+    barrier = pltpu.get_barrier_semaphore()
+
+    @pl.loop(0, peers - 1)
+    def _(i):
+        pl.semaphore_signal(barrier, inc=1, device_id={"replica": target(i)}, device_id_type=MESH)
+
     home_local.start()
     ids_copy.start()
     x_copy.start()
-    barrier = pltpu.get_barrier_semaphore()
-
-    @pl.loop(0, peers - 1)
-    def _(i):
-        pl.semaphore_signal(barrier, inc=1, device_id={"replica": target(i)}, device_id_type=MESH)
-
-    for c in range(w_parts):
-        w_copy(c).start()
-    shrink_copy.start()
-    k_copy.start()
-    v_copy.start()
-    len_copy.start()
-    expand_copy.start()
+
     home_local.wait()
     home_src[...] = jnp.full(home_src.shape, home_ref[0], jnp.int32)
     homes[me] = home_src[...]
@@ -131,6 +125,14 @@
     @pl.loop(0, peers - 1)
     def _(i):
         home_copy(i, me).start()
+
+    for c in range(w_parts):
+        w_copy(c).start()
+    shrink_copy.start()
+    k_copy.start()
+    v_copy.start()
+    len_copy.start()
+    expand_copy.start()
 
     total = steps * rows
     ids_copy.wait()
@@ -186,14 +188,18 @@
     for s in range(steps):
         routing = jnp.where(fits[s] & (pack_target == owner_of(pack_ids[s])), 1.0, 0.0).astype(BF16)
         tall = jnp.concatenate([x[s, :, c * cols : (c + 1) * cols] for c in range(parts)], axis=0)
-        packed = jnp.dot(routing, tall, preferred_element_type=F32).astype(BF16)
-        packed = packed.reshape(peers, 16, cols)
-        out[:, s * 16 : (s + 1) * 16, :] = packed
-        inbox[peers - 1, s * 16 : (s + 1) * 16, :] = packed[peers - 1]
-
-        @pl.loop(0, peers - 1)
-        def _(i):
-            row_copy(s, i).start()
+        for g in range(2):
+            packed = jnp.dot(
+                routing[g * half * 16 : (g + 1) * half * 16], tall, preferred_element_type=F32
+            ).astype(BF16)
+            packed = packed.reshape(half, 16, cols)
+            out[g * half : (g + 1) * half, s * 16 : (s + 1) * 16, :] = packed
+            if g == 1:
+                inbox[peers - 1, s * 16 : (s + 1) * 16, :] = packed[half - 1]
+
+            @pl.loop(g * half, min((g + 1) * half, peers - 1))
+            def _(i):
+                row_copy(s, i).start()
 
     q_lanes = iota((1, rows * per_row), 1)
     q_rows = q_lanes // per_row + ((q_lanes // heads) % steps) * rows
@@ -271,7 +277,7 @@
     spread = jnp.where(spread, 1.0, 0.0).astype(BF16)
     own_head = iota((r_rows, heads * rank), 0) % heads == iota((r_rows, heads * rank), 1) // rank
     for s in range(steps):
-        for g in range(2):
+        for g in (0, 1):
             wait_rows(s, g)
             lows[s, g] = low_rank(s, g)
             if s < steps - 1:
@@ -289,6 +295,13 @@
             @pl.loop(g * half, min((g + 1) * half, peers - 1))
             def _(i):
                 answer_copy(i, source(i)).start()
+
+    @pl.loop(0, peers - 1)
+    def _(i):
+        home_copy(i, me).wait_send()
+        for s in range(steps):
+            row_copy(s, i).wait_send()
+        answer_copy(i, source(i)).wait_send()
 
     @pl.loop(0, peers - 1)
     def _(i):
@@ -308,13 +321,6 @@
             o_ref[s, :, h * HEAD : (h + 1) * HEAD] = mixed[
                 pl.ds(s * heads + h, rows, stride=per_row), :
             ].astype(BF16)
-
-    @pl.loop(0, peers - 1)
-    def _(i):
-        home_copy(i, me).wait_send()
-        for s in range(steps):
-            row_copy(s, i).wait_send()
-        answer_copy(i, source(i)).wait_send()
 
 
 def body(inputs, query_weight, key_cache, value_cache, cache_len, ids, home, shrink_pool, expand_pool):
@@ -345,8 +351,8 @@
             pltpu.VMEM((1, rank, width), BF16),
             pltpu.VMEM(expand_pool.shape, BF16),
             pltpu.VMEM((rank * 16 // MOST, cols), BF16),
-            pltpu.VMEM((8, 128), jnp.int32),
-            pltpu.VMEM((peers, 8, 128), jnp.int32),
+            pltpu.VMEM((1, 128), jnp.int32),
+            pltpu.VMEM((peers, 1, 128), jnp.int32),
             pltpu.VMEM((peers, steps * 16, cols), BF16),
             pltpu.VMEM((peers, steps * 16, cols), BF16),
             pltpu.VMEM((peers, steps * MOST * heads, HEAD), BF16),

time: 45.2 us -> 44.5 us (0.985)
  Pallas kernels: 42.9 us -> 42.2 us
    pallas_call x1, Pallas kernels: 42.9 us -> 42.2 us  [body(): pl.pallas_call(functools.partial(kernel, peers, steps, rows, width, rank,...]
where the time goes in v3:
time: 44.5 us; the launch traced here: 44.3 us
  Pallas kernels  42.2 us (95%)
  local copies, waits for them, and re-layouts  1.47 us (3%)
  between operations  0.66 us (1%)
    pallas_call x1, Pallas kernels, body(): pl.pallas_call(functools.partial(kernel, peers, steps, rows, width, rank,...  42.2 us
    unnamed x1, local copies, waits for them, and re-layouts  1.47 us

profile of v3, /device:TPU:0, one launch (start us, length us, event | category | flops | bytes accessed | tf_op | source)
XLA Modules:
  0.0 44.3 jit_solution(7046029534278458689)
XLA Ops:
  0.7 42.2 %shard_map.91 = bf16[2,32,512]{2,1,0:T(8,128)(2,1)} custom-call(bf16[2,32,8192]{2,1,0:T(8,128)(2,1)} %x_hbm.1, bf16[8192,512]{1,0:T(8,128)(2,1)} %w_hbm.1, bf16[32,128,128]{2,1,0:T(8,128)(2,1)} %k_hbm.1, bf16[32,128,128]{2,1,0:T(8,128)(2,1)} %v_hbm.1, s32[32]{0:T(128)} %len_hbm.1, s32[2,1,32]{2,1,0:T(1,128)} %bitcast.5, s32[1]{0:T(128)S(6)} %copy.12.home_hbm, ...), custom_call_target="tpu_custom_call" | custom-call | tf_op jit(solution)/shard_map/pallas_call | solution.py:338
  42.8 1.5 %copy.13 = bf16[2,32,512]{2,1,0:T(8,128)(2,1)} copy(bf16[2,32,512]{2,1,0:T(8,128)(2,1)} %shard_map.91) | data formatting | bytes 131072

commit v4 on v3

--- a/solution.py
+++ b/solution.py
@@ -69,7 +69,7 @@
     parts = 16 // MOST
     cols = width // parts
     per_row = steps * heads
-    half = peers // 2
+    share = peers
     w_parts = w_sem.shape[0]
     w_rows = width // w_parts
 
@@ -188,16 +188,16 @@
     for s in range(steps):
         routing = jnp.where(fits[s] & (pack_target == owner_of(pack_ids[s])), 1.0, 0.0).astype(BF16)
         tall = jnp.concatenate([x[s, :, c * cols : (c + 1) * cols] for c in range(parts)], axis=0)
-        for g in range(2):
+        for g in range(1):
             packed = jnp.dot(
-                routing[g * half * 16 : (g + 1) * half * 16], tall, preferred_element_type=F32
+                routing[g * share * 16 : (g + 1) * share * 16], tall, preferred_element_type=F32
             ).astype(BF16)
-            packed = packed.reshape(half, 16, cols)
-            out[g * half : (g + 1) * half, s * 16 : (s + 1) * 16, :] = packed
-            if g == 1:
-                inbox[peers - 1, s * 16 : (s + 1) * 16, :] = packed[half - 1]
-
-            @pl.loop(g * half, min((g + 1) * half, peers - 1))
+            packed = packed.reshape(share, 16, cols)
+            out[g * share : (g + 1) * share, s * 16 : (s + 1) * 16, :] = packed
+            if g == 0:
+                inbox[peers - 1, s * 16 : (s + 1) * 16, :] = packed[share - 1]
+
+            @pl.loop(g * share, min((g + 1) * share, peers - 1))
             def _(i):
                 row_copy(s, i).start()
 
@@ -238,11 +238,11 @@
     k_copy.wait()
     v_copy.wait()
 
-    g_rows = half * 16
+    g_rows = share * 16
     own_part = iota((g_rows, parts * rank), 0) % parts == iota((g_rows, parts * rank), 1) // rank
 
     def low_rank(s, g):
-        block = inbox[g * half : (g + 1) * half, s * 16 : (s + 1) * 16, :].reshape(g_rows, cols)
+        block = inbox[g * share : (g + 1) * share, s * 16 : (s + 1) * 16, :].reshape(g_rows, cols)
         full = lax.dot_general(block, wide[...], (((1,), (1,)), ((), ())), preferred_element_type=F32)
         full = jnp.where(own_part, full, 0.0).reshape(g_rows // parts, parts, parts * rank)
         full = jnp.sum(full, axis=1)
@@ -251,7 +251,7 @@
         return (full + pltpu.roll(full, rank, 1)).astype(BF16)
 
     def wait_rows(s, g):
-        @pl.loop(g * half, min((g + 1) * half, peers - 1))
+        @pl.loop(g * share, min((g + 1) * share, peers - 1))
         def _(i):
             row_copy(s, i).wait_recv()
 
@@ -266,18 +266,18 @@
         )
 
     lows = {}
-    r_rows = half * per_peer
-    r_from = iota((r_rows, steps * half * MOST), 1)
-    r_to = iota((r_rows, steps * half * MOST), 0)
+    r_rows = share * per_peer
+    r_from = iota((r_rows, steps * share * MOST), 1)
+    r_to = iota((r_rows, steps * share * MOST), 0)
     spread = (
-        ((r_to // (MOST * heads)) % steps == r_from // (half * MOST))
-        & (r_to // per_peer == (r_from // MOST) % half)
+        ((r_to // (MOST * heads)) % steps == r_from // (share * MOST))
+        & (r_to // per_peer == (r_from // MOST) % share)
         & ((r_to // heads) % MOST == r_from % MOST)
     )
     spread = jnp.where(spread, 1.0, 0.0).astype(BF16)
     own_head = iota((r_rows, heads * rank), 0) % heads == iota((r_rows, heads * rank), 1) // rank
     for s in range(steps):
-        for g in (0, 1):
+        for g in range(1):
             wait_rows(s, g)
             lows[s, g] = low_rank(s, g)
             if s < steps - 1:
@@ -287,12 +287,12 @@
             low = jnp.dot(spread, low, preferred_element_type=F32)
             low = jnp.where(own_head, low, 0.0).astype(BF16)
             answer = jnp.dot(low, expand_tall, preferred_element_type=F32).astype(BF16)
-            answer = answer.reshape(half, per_peer, HEAD)
-            ans_out[g * half : (g + 1) * half] = answer
-            if g == 1:
-                ans_in[peers - 1] = answer[half - 1]
-
-            @pl.loop(g * half, min((g + 1) * half, peers - 1))
+            answer = answer.reshape(share, per_peer, HEAD)
+            ans_out[g * share : (g + 1) * share] = answer
+            if g == 0:
+                ans_in[peers - 1] = answer[share - 1]
+
+            @pl.loop(g * share, min((g + 1) * share, peers - 1))
             def _(i):
                 answer_copy(i, source(i)).start()
 

time: 44.5 us -> 43.8 us (0.984)
  Pallas kernels: 42.2 us -> 41.5 us
    pallas_call x1, Pallas kernels: 42.2 us -> 41.5 us  [body(): pl.pallas_call(functools.partial(kernel, peers, steps, rows, width, rank,...]
where the time goes in v4:
time: 43.8 us; the launch traced here: 43.7 us
  Pallas kernels  41.5 us (95%)
  local copies, waits for them, and re-layouts  1.47 us (3%)
  between operations  0.66 us (2%)
    pallas_call x1, Pallas kernels, body(): pl.pallas_call(functools.partial(kernel, peers, steps, rows, width, rank,...  41.5 us
    unnamed x1, local copies, waits for them, and re-layouts  1.47 us

profile of v4, /device:TPU:0, one launch (start us, length us, event | category | flops | bytes accessed | tf_op | source)
XLA Modules:
  0.0 43.7 jit_solution(4131136921378827094)
XLA Ops:
  0.7 41.5 %shard_map.91 = bf16[2,32,512]{2,1,0:T(8,128)(2,1)} custom-call(bf16[2,32,8192]{2,1,0:T(8,128)(2,1)} %x_hbm.1, bf16[8192,512]{1,0:T(8,128)(2,1)} %w_hbm.1, bf16[32,128,128]{2,1,0:T(8,128)(2,1)} %k_hbm.1, bf16[32,128,128]{2,1,0:T(8,128)(2,1)} %v_hbm.1, s32[32]{0:T(128)} %len_hbm.1, s32[2,1,32]{2,1,0:T(1,128)} %bitcast.5, s32[1]{0:T(128)S(6)} %copy.12.home_hbm, ...), custom_call_target="tpu_custom_call" | custom-call | tf_op jit(solution)/shard_map/pallas_call | solution.py:338
  42.2 1.5 %copy.13 = bf16[2,32,512]{2,1,0:T(8,128)(2,1)} copy(bf16[2,32,512]{2,1,0:T(8,128)(2,1)} %shard_map.91) | data formatting | bytes 131072
